TPU v7x, 32 devices: a whole 2x2x4 slice. The times are simulated.
32 devices in a mesh: blk: 2 (over x), pair: 16 (over z, y, core).
Axes of the slice: x: 2, y: 2, z: 4, core: 2. Of those that a mesh axis runs over, the one named last changes fastest.
Arguments:
- panels: bfloat16 [96, 384, 1152], P('pair', None, 'blk'), may hold values from -1 to 1
- pattern: int32 [96, 2], P('pair', 'blk'), may hold values 0 or 1
- point_inverse: float32 [96, 9, 128], P('pair'), as said below
- camera_hessian: float32 [1152, 576], P('blk'), as said below
- damping: int32 [1152], P('blk'), may hold values from 0 to 3
- camera_grad: float32 [1152], P('blk'), may hold values from -6 to 6
- point_grad: float32 [96, 384], P('pair'), may hold values from -6 to 6
Outputs:
- schur: float32 [1152, 1152], P('pair', 'blk')
- reduced_rhs: float32 [1152], P('blk')
Inputs may be any that keep to these rules, and one draw needn't show every extreme that they name: point_inverse is symmetric in its 3 x 3 entries with a positive diagonal. camera_hessian blocks are symmetric with a positive diagonal.
All inputs are finite; a program needn't handle non-finite values. No bound on the sum of `pattern` on one device may be relied on, other than what follows from the above.
Results may differ from a plain program's by a relative error of at most 0.003.
Values may be sent and summed in bfloat16 or wider, within the bound.
A program may use at most 128 MiB of HBM per device.

v0:
```python
import jax
import jax.numpy as jnp
from jax import lax
from jax.sharding import PartitionSpec as P


def apply_inverse(inverse, shaped):
    parts = []
    for row in range(3):
        total = inverse[:, row * 3, :, None] * shaped[:, 0]
        total = total + inverse[:, row * 3 + 1, :, None] * shaped[:, 1]
        total = total + inverse[:, row * 3 + 2, :, None] * shaped[:, 2]
        parts.append(total)
    return jnp.stack(parts, axis=1)


def shards(panels, pattern, point_inverse, camera_hessian, damping, camera_grad, point_grad):
    block_count = panels.shape[0]
    camera_width = panels.shape[2]
    point_count = point_inverse.shape[2]
    panel_rows = block_count * 3 * point_count
    masked = panels * pattern.astype(jnp.bfloat16)[:, :, None]
    shaped = masked.astype(jnp.float32).reshape(block_count, 3, point_count, camera_width)
    scaled = (
        apply_inverse(point_inverse, shaped).astype(jnp.bfloat16).reshape(panel_rows, camera_width)
    )
    flat_panels = masked.reshape(panel_rows, camera_width)
    my_block = lax.axis_index("blk")
    gathered = lax.all_gather(scaled, "blk", axis=1, tiled=True)
    total_rows = gathered.shape[1]
    owners = lax.axis_size("pair")
    own_rows = total_rows // owners
    piece = lax.psum_scatter(
        -lax.dot_general(
            gathered, flat_panels, (((0,), (0,)), ((), ())), preferred_element_type=jnp.float32
        ),
        "pair",
        scatter_dimension=0,
        tiled=True,
    )
    diag_vals = jnp.diagonal(camera_hessian)
    levels = 0.1 * jnp.power(2.0, damping.astype(jnp.float32))
    damped = (
        camera_hessian + jnp.eye(camera_width, dtype=jnp.float32) * (levels * diag_vals)[:, None]
    )
    row_start = lax.axis_index("pair") * own_rows
    offset = jnp.clip(row_start - my_block * camera_width, 0, camera_width - own_rows)
    hessian_rows = lax.dynamic_slice_in_dim(damped, offset, own_rows, 0)
    inside = row_start // camera_width == my_block
    schur = piece + jnp.where(inside, hessian_rows, jnp.zeros_like(hessian_rows))
    grads = point_grad.reshape(block_count, 3, point_count)
    point_step = apply_inverse(point_inverse, grads[:, :, :, None])[..., 0]
    point_step = point_step.astype(jnp.bfloat16).reshape(panel_rows)
    local_terms = jnp.dot(point_step, flat_panels, preferred_element_type=jnp.float32)
    summed = lax.psum(local_terms, "pair")
    reduced_rhs = camera_grad - summed
    return (schur, reduced_rhs)


def solution(mesh):
    return jax.shard_map(
        shards,
        mesh=mesh,
        in_specs=(
            P("pair", None, "blk"),
            P("pair", "blk"),
            P("pair", None, None),
            P("blk", None),
            P("blk"),
            P("blk"),
            P("pair", None),
        ),
        out_specs=(P("pair", "blk"), P("blk")),
        check_vma=False,
    )
```

profile of v0, /device:TPU:0, one launch (start us, length us, event | category | flops | bytes accessed | tf_op | source)
XLA Modules:
  0.0 181.3 jit_solution(9461285882114132046)
XLA Ops:
  7.2 0.0 all-gather.2.cloned.1.call-start
  7.2 0.8 slice_bitcast_fusion.8
  8.0 0.7 convert_bitcast_fusion
  8.7 2.1 %broadcast_multiply_fusion = bf16[6,384,576]{1,2,0:T(8,128)(2,1)S(1)} fusion(bf16[6,384,576]{1,2,0:T(8,128)(2,1)} %param.7, bf16[6]{0:T(256)(128)(2,1)S(1)} %convert_bitcast_fusion), kind=kLoop, calls=%fused_computation.6 | loop fusion | flops 1327104 | bytes 5308428 | tf_op jit(solution)/shard_map/mul | solution.py:22
  10.8 4.4 %copy.15 = f32[6,384,576]{2,1,0:T(8,128)} copy(bf16[6,384,576]{1,2,0:T(8,128)(2,1)S(1)} %broadcast_multiply_fusion) | data formatting | bytes 7962624 | tf_op jit(solution)/shard_map/reshape | solution.py:23
  15.2 3.9 %add_convert_fusion.2 = (bf16[6,1,128,576]{3,2,1,0:T(8,128)(2,1)S(1)}, bf16[6,1,128,576]{3,2,1,0:T(8,128)(2,1)S(1)}, bf16[6,1,128,576]{3,2,1,0:T(8,128)(2,1)S(1)}) fusion(f32[6,3,128,576]{3,2,1,0:T(8,128)} %bitcast.79, f32[6,128]{1,0:T(8,128)S(1)} %get-tuple-element.13, f32[6,128]{1,0:T(8,128)S(1)} %get-tuple-element.14, f32[6,128]{1,0:T(8,128)S(1)} %get-tuple-element.8, ...), kind=kLoop, calls=%fused_computation.5 | loop fusion | flops 7962624 | bytes 7990272 | tf_op jit(solution)/shard_map/convert.4
  19.1 2.1 %pad_maximum_fusion = bf16[6,3,128,576]{3,2,1,0:T(8,128)(2,1)} fusion(bf16[6,1,128,576]{3,2,1,0:T(8,128)(2,1)S(1)} %get-tuple-element.4, bf16[6,1,128,576]{3,2,1,0:T(8,128)(2,1)S(1)} %get-tuple-element.3, bf16[6,1,128,576]{3,2,1,0:T(8,128)(2,1)S(1)} %get-tuple-element.2), kind=kLoop, calls=%fused_computation.2 | loop fusion | flops 2654208 | bytes 5308416 | tf_op jit(solution)/shard_map/stack | solution.py:14
  21.2 4.5 %copy.16 = bf16[2304,576]{0,1:T(8,128)(2,1)} copy(bf16[2304,576]{1,0:T(8,128)(2,1)} %bitcast.82) | data formatting | bytes 5308416 | tf_op jit(solution)/shard_map/convert_element_type | solution.py:25
  25.8 0.0 all-gather.2.cloned.1.call-update
  25.8 0.0 reduce-scatter.4.cloned.1.call-start
  25.8 3.7 %copy.17 = bf16[6,384,576]{2,1,0:T(8,128)(2,1)} copy(bf16[6,384,576]{1,2,0:T(8,128)(2,1)S(1)} %broadcast_multiply_fusion) | data formatting | bytes 5308416 | tf_op jit(solution)/shard_map/mul | solution.py:22
  29.6 68.4 %all-gather.2.cloned.1.call-done = bf16[2304,1152]{0,1:T(8,128)(2,1)} async-done(((bf16[2304,576]{0,1:T(8,128)(2,1)}), bf16[2304,1152]{0,1:T(8,128)(2,1)}) %all-gather.2.cloned.1.call-update) | async-done | bytes 5308432 | tf_op jit(solution)/shard_map/all_gather | solution.py:29
  97.9 9.4 %convolution_negate_fusion = f32[1152,576]{1,0:T(8,128)} fusion(bf16[2304,1152]{0,1:T(8,128)(2,1)} %all-gather.2.cloned.1.call-done, bf16[2304,576]{1,0:T(8,128)(2,1)} %bitcast.80), kind=kOutput, calls=%fused_computation.1 | convolution fusion | flops 3058311168 | bytes 10616832 | tf_op jit(solution)/shard_map/dot_general | solution.py:34
  107.3 0.0 copy-start.1
  107.3 0.0 copy-start.2
  107.3 0.0 copy-start
  107.3 0.0 reduce-scatter.4.cloned.1.call-update
  107.4 0.7 copy-done.1
  108.1 0.0 copy-done.2
  108.2 0.5 copy-done
  108.7 0.0 copy-start.3
  108.7 4.9 %gather_fusion = f32[576]{0:T(1024)S(1)} fusion(f32[576,576]{1,0:T(8,128)S(1)} %copy-done, s32[576]{0:T(1024)S(1)} %or_reduce_fusion), kind=kCustom, calls=%fused_computation | custom fusion | bytes 9216 | tf_op jit(solution)/shard_map/jit(diagonal)/cond/branch_0_fun/gather | solution.py:41
  113.7 0.0 copy-done.3
  113.7 0.0 copy-start.4
  113.7 0.1 dynamic-slice.2
  113.8 2.5 %convolution_reduce_fusion = f32[576]{0:T(1024)S(1)} fusion(bf16[2304,1]{0,1:T(2,128)(2,1)S(1)} %reshape.137, bf16[2304,576]{1,0:T(8,128)(2,1)} %bitcast.81), kind=kOutput, calls=%fused_computation.7 | convolution fusion | flops 2654208 | bytes 2661120 | tf_op jit(solution)/shard_map/dot_general | solution.py:54
  116.3 33.6 %psum.7 = f32[576]{0:T(1024)S(1)} all-reduce(f32[576]{0:T(1024)S(1)} %convolution_reduce_fusion), channel_id=1, replica_groups=mesh['blk'=2,'pair'=16] {'pair'}, use_global_device_ids=true, to_apply=%region_1.2 | all-reduce | flops 576 | bytes 4608 | tf_op jit(solution)/shard_map/psum | solution.py:55
  149.9 0.0 copy-done.4
  149.9 0.6 sub.12
  150.5 22.3 %reduce-scatter.4.cloned.1.call-done = f32[72,576]{1,0:T(8,128)} async-done(((f32[1152,576]{1,0:T(8,128)}), f32[72,576]{1,0:T(8,128)}) %reduce-scatter.4.cloned.1.call-update) | async-done | bytes 165904
  172.8 1.7 fusion.1
  (6 shorter events, 0.1 us)
Async XLA Ops:
  7.2 90.8 %all-gather.2.cloned.1.call-start = ((), (), s32[]{:S(2)}) async-start(), calls=%async_computation.1 | async-start | bytes 7962624 | tf_op jit(solution)/shard_map/all_gather | solution.py:29
  25.8 147.0 %reduce-scatter.4.cloned.1.call-start = ((), (), s32[]{:S(2)}) async-start(), calls=%async_computation.2 | async-start | bytes 3133440
  107.3 0.8 copy-start.1
  107.3 0.8 copy-start.2
  107.3 1.4 copy-start
  108.7 4.9 %copy-start.3 = (s32[576]{0:T(1024)S(1)}, s32[576]{0:T(1024)}, u32[]{:S(2)}) copy-start(s32[576]{0:T(1024)} %param.11) | copy-start | bytes 6916
  113.7 36.2 %copy-start.4 = (f32[576]{0:T(1024)S(1)}, f32[576]{0:T(1024)}, u32[]{:S(2)}) copy-start(f32[576]{0:T(1024)} %param.12) | copy-start | bytes 6916
Sparse Core Ops, SparseCore 0:
  25.9 71.9 all-gather.1
  107.5 65.2 reduce-scatter.3
where the time goes:
time: 182 us; the launch traced here: 181 us
  waiting for transfers between devices  90.7 us (50%)
  blocking collectives  33.6 us (18%)
  local copies, waits for them, and re-layouts  19.8 us (11%)
  between operations  14.1 us (8%)
  matrix products  11.9 us (7%)
  other arithmetic  11.1 us (6%)
    all_gather x1, waiting for transfers between devices, shards(): gathered = lax.all_gather(scaled, 'blk', axis=1, tiled=True)  68.4 us
    psum x1, blocking collectives, shards(): summed = lax.psum(local_terms, 'pair')  33.6 us
    unnamed x3, waiting for transfers between devices  22.3 us
    dot_general x1, matrix products, shards(): lax.dot_general(gathered, flat_panels, (((0,), (0,)), ((), ())), preferre...  9.4 us
    gather x1, local copies, waits for them, and re-layouts, shards(): diag_vals = jnp.diagonal(camera_hessian)  4.93 us
    convert_element_type x1, local copies, waits for them, and re-layouts, shards(): apply_inverse(point_inverse, shaped).astype(jnp.bfloat16)  4.53 us
    reshape x1, local copies, waits for them, and re-layouts, shards(): masked.astype(jnp.float32)  4.44 us
    another operation x2, other arithmetic  3.94 us
  transfers between devices with their start and end apart: 2, of which 2 were waited for; matrix products, arithmetic and copies ran while one was open for 7% of the time, Pallas kernels for 0%

commit v1 on v0

v1 whole, which is shorter than its diff:
```python
import functools

import jax
import jax.numpy as jnp
import numpy as np
from jax import lax
from jax.experimental import pallas as pl
from jax.experimental.pallas import tpu as pltpu
from jax.sharding import PartitionSpec as P

MESH = pl.DeviceIdType.MESH
LANES = 128
F32 = jnp.float32
BF16 = jnp.bfloat16


def apply_inverse(inverse, shaped):
    parts = []
    for row in range(3):
        total = inverse[:, row * 3, :, None] * shaped[:, 0]
        total = total + inverse[:, row * 3 + 1, :, None] * shaped[:, 1]
        total = total + inverse[:, row * 3 + 2, :, None] * shaped[:, 2]
        parts.append(total)
    return jnp.stack(parts, axis=1)


def finish(piece, summed, camera_hessian, damping, camera_grad, own_rows):
    camera_width = camera_hessian.shape[1]
    row_start = lax.axis_index("pair") * own_rows
    first = row_start - lax.axis_index("blk") * camera_width
    inside = (first >= 0) & (first < camera_width)
    offset = jnp.clip(first, 0, camera_width - own_rows)
    rows = lax.dynamic_slice_in_dim(camera_hessian, offset, own_rows, 0)
    levels = 0.1 * lax.shift_left(jnp.ones_like(damping), damping).astype(F32)
    row_at = lax.broadcasted_iota(jnp.int32, rows.shape, 0) + offset
    col_at = lax.broadcasted_iota(jnp.int32, rows.shape, 1)
    damped = rows + jnp.where(row_at == col_at, levels[None, :] * rows, 0.0)
    schur = jnp.where(inside, damped, 0.0) - piece
    return schur, camera_grad - summed


def general_shards(panels, pattern, point_inverse, camera_hessian, damping, camera_grad, point_grad):
    block_count = panels.shape[0]
    camera_width = panels.shape[2]
    point_count = point_inverse.shape[2]
    panel_rows = block_count * 3 * point_count
    masked = panels * pattern.astype(BF16)[:, :, None]
    shaped = masked.astype(F32).reshape(block_count, 3, point_count, camera_width)
    scaled = apply_inverse(point_inverse, shaped).astype(BF16).reshape(panel_rows, camera_width)
    flat_panels = masked.reshape(panel_rows, camera_width)
    gathered = lax.all_gather(scaled, "blk", axis=1, tiled=True)
    own_rows = gathered.shape[1] // lax.axis_size("pair")
    piece = lax.psum_scatter(
        lax.dot_general(gathered, flat_panels, (((0,), (0,)), ((), ())), preferred_element_type=F32),
        "pair",
        scatter_dimension=0,
        tiled=True,
    )
    grads = point_grad.reshape(block_count, 3, point_count)
    point_step = apply_inverse(point_inverse, grads[:, :, :, None])[..., 0]
    point_step = point_step.astype(BF16).reshape(panel_rows)
    local_terms = jnp.dot(point_step, flat_panels, preferred_element_type=F32)
    summed = lax.psum(local_terms, "pair")
    return finish(piece, summed, camera_hessian, damping, camera_grad, own_rows)


def column_order(width, slabs, group):
    own = width // slabs
    full, rest = own // group, own % group
    hot = np.zeros((width, (full + 2) * LANES), np.float32)
    for c in range(full):
        for s in range(slabs):
            for r in range(group):
                hot[s * own + c * group + r, c * LANES + s * group + r] = 1
    for s in range(slabs):
        for r in range(rest):
            at = s * own + full * group + r
            hot[at, full * LANES + s * rest + r] = 1
            hot[at, (full + 1) * LANES + slabs * rest + s * rest + r] = 1
    return hot


class Names:
    def __init__(self):
        self.order, self.shapes = {}, []

    def add(self, name, shape):
        self.order[name] = len(self.shapes)
        self.shapes.append(shape)


def tdot(a, b):
    return lax.dot_general(a, b, (((0,), (0,)), ((), ())), preferred_element_type=F32)


def plan(nk, rows, width, slabs, own, group):
    full, rest = own // group, own % group
    stages = slabs.bit_length() - 1
    half = nk // 2 * rows
    names = Names()
    items = [[("d", own, width)]]
    for c in range(full):
        items.append([("t%d" % c, group, width), ("u%d" % c, own, LANES)])
    items.append([("t%d" % full, rest, width), ("u%d" % full, own, LANES)])
    copies = 0
    for item in items:
        for tag, r, w in item:
            n = slabs
            names.add(tag + "a0", pltpu.VMEM((n, r, w), F32))
            for i in range(stages):
                n //= 2
                names.add(tag + "s%d" % i, pltpu.VMEM((n * r, w), BF16))
                names.add(tag + "r%d" % i, pltpu.VMEM((n * r, w), BF16))
                names.add(tag + "a%d" % (i + 1), pltpu.VMEM((n, r, w), F32))
            names.add(tag + "s%d" % stages, pltpu.VMEM((r, w), BF16))
            names.add(tag + "r%d" % stages, pltpu.VMEM((r, w), BF16))
            if tag[0] == "u":
                names.add(tag + "sx", pltpu.VMEM((r, w), BF16))
                names.add(tag + "rx", pltpu.VMEM((r, w), BF16))
    for i in range(stages + 1):
        names.add("hs%d" % i, pltpu.VMEM((8, width), F32))
        names.add("hr%d" % i, pltpu.VMEM((8, width), F32))
    for c in range(full + 1):
        deep = half if c < full else half // 2
        names.add("xs%d" % c, pltpu.VMEM((deep, LANES), BF16))
        names.add("xr%d" % c, pltpu.VMEM((deep, LANES), BF16))
    names.add("scaled", pltpu.VMEM((nk, rows, width), BF16))
    names.add("mine", pltpu.VMEM((half, width), BF16))
    names.add("total", pltpu.VMEM((width, width), F32))
    count = len(names.shapes)
    names.add("send", pltpu.SemaphoreType.DMA((count,)))
    names.add("recv", pltpu.SemaphoreType.DMA((count,)))
    return names, items, stages, full, rest


def kernel(names, items, stages, full, rest, slabs, group, pattern, panels, inverse, grads, hot, piece, rhs, *refs):
    at = lambda name: refs[names.order[name]]
    nk, rows, width = panels.shape
    points = rows // 3
    half = nk // 2 * rows
    own = width // slabs
    blk = lax.axis_index("blk")
    pair = lax.axis_index("pair")
    bit = [lax.rem(lax.div(pair, 2**i), 2) for i in range(stages + 1)]
    mate = [{"pair": pair + (1 - 2 * bit[i]) * 2**i} for i in range(stages + 1)]
    across = {"blk": 1 - blk}
    top = bit[stages]
    owns_diag = top == blk
    owns_off = top != blk

    barrier = pltpu.get_barrier_semaphore()
    for other in mate + [across]:
        pl.semaphore_signal(barrier, inc=1, device_id=other, device_id_type=MESH)

    def copy(src, dst, other):
        n = names.order[src]
        return pltpu.make_async_remote_copy(
            src_ref=at(src),
            dst_ref=at(dst),
            send_sem=at("send").at[n],
            recv_sem=at("recv").at[n],
            device_id=other,
            device_id_type=MESH,
        )

    def xcopy(c):
        return copy("xs%d" % c, "xr%d" % c, across)

    def hop(tag, i):
        return copy(tag + "s%d" % i, tag + "r%d" % i, mate[i])

    def ucopy(tag):
        return copy(tag + "sx", tag + "rx", across)

    first = blk * (nk // 2)
    other_first = (1 - blk) * (nk // 2)
    for j in range(nk // 2):
        seen = pattern[first + j, 0].astype(F32)
        at("mine")[pl.ds(j * rows, rows), :] = (panels[first + j].astype(F32) * seen).astype(BF16)

    def fill(c):
        if c < full:
            columns = hot[:, pl.ds(c * LANES, LANES)]
            at("xs%d" % c)[...] = jnp.dot(at("mine")[...], columns, preferred_element_type=F32).astype(BF16)
        else:
            low = hot[:, pl.ds(full * LANES, LANES)]
            high = hot[:, pl.ds((full + 1) * LANES, LANES)]
            upper = at("mine")[pl.ds(0, half // 2), :]
            lower = at("mine")[pl.ds(half // 2, half // 2), :]
            packed = jnp.dot(upper, low, preferred_element_type=F32)
            packed = packed + jnp.dot(lower, high, preferred_element_type=F32)
            at("xs%d" % c)[...] = packed.astype(BF16)

    fill(0)
    pl.semaphore_wait(barrier, len(mate) + 1)
    xcopy(0).start()
    for c in range(1, full + 1):
        fill(c)
        if c == 1:
            xcopy(c).start()

    at("total")[...] = jnp.zeros((width, width), F32)
    at("hs0")[...] = jnp.zeros((8, width), F32)
    piece[...] = jnp.zeros_like(piece)

    def block(k, carry):
        seen = pattern[k, 0].astype(F32)
        masked = (panels[k].astype(F32) * seen).astype(BF16)
        wide = masked.astype(F32)
        flat = inverse[k]
        tall = jnp.concatenate([flat, jnp.zeros((16 - 9, points), F32)], axis=0).T
        picked = lax.broadcasted_iota(jnp.int32, grads.shape, 0) == k
        grad = jnp.sum(jnp.where(picked, grads[...], 0.0), axis=0, keepdims=True)
        parts, steps = [], []
        for a in range(3):
            total, step = None, None
            for c in range(3):
                n = a * 3 + c
                term = tall[:, n : n + 1] * wide[c * points : (c + 1) * points]
                part = flat[n : n + 1] * grad[:, c * points : (c + 1) * points]
                total = term if total is None else total + term
                step = part if step is None else step + part
            parts.append(total.astype(BF16))
            steps.append(step)
        for a in range(3):
            at("scaled")[k, pl.ds(a * points, points), :] = parts[a]
        at("total")[...] += tdot(at("scaled")[k], masked)
        stepped = jnp.broadcast_to(jnp.concatenate(steps, axis=1), (8, rows)).astype(BF16)
        at("hs0")[...] += jnp.dot(stepped, masked, preferred_element_type=F32)
        return carry

    lax.fori_loop(0, nk, block, 0)

    def held():
        return at("scaled")[pl.ds(other_first, nk // 2)].reshape(half, width)

    def produce(n):
        if n == 0:
            at("da0")[...] = at("total")[...].reshape(slabs, own, width)
            return
        c = n - 1
        xcopy(c).wait_recv()
        if c + 2 <= full:
            xcopy(c + 2).start()
        got = at("xr%d" % c)[...]
        mix = held()
        if c < full:
            at("t%da0" % c)[...] = tdot(got, mix).reshape(slabs, group, width)
            at("u%da0" % c)[...] = tdot(mix, got).reshape(slabs, own, LANES)
        else:
            packed = slabs * rest
            upper, lower = mix[: half // 2], mix[half // 2 :]
            both = tdot(got, upper)[:packed] + tdot(got, lower)[packed : 2 * packed]
            at("t%da0" % c)[...] = both.reshape(slabs, rest, width)
            lane = lax.broadcasted_iota(jnp.int32, (width, LANES), 1)
            side = jnp.where(lane < packed, tdot(upper, got), tdot(lower, got))
            at("u%da0" % c)[...] = side.reshape(slabs, own, LANES)

    def push(n, i):
        for tag, r, w in items[n]:
            acc = at(tag + "a%d" % i)
            if i < stages:
                count = slabs >> (i + 1)
                cast = [acc[2 * m + 1 - bit[i]].astype(BF16) for m in range(count)]
                for m in range(count):
                    at(tag + "s%d" % i)[pl.ds(m * r, r), :] = cast[m]
                hop(tag, i).start()
            else:
                at(tag + "s%d" % i)[...] = acc[0].astype(BF16)

                @pl.when(owns_diag if tag[0] == "t" else owns_off)
                def _():
                    hop(tag, i).start()
        if n == 0:
            hop("h", i).start()

    def pull(n, i):
        for tag, r, w in items[n]:
            acc = at(tag + "a%d" % i)
            if i < stages:
                hop(tag, i).wait_recv()
                for m in range(slabs >> (i + 1)):
                    got = at(tag + "r%d" % i)[pl.ds(m * r, r), :].astype(F32)
                    at(tag + "a%d" % (i + 1))[m] = acc[2 * m + bit[i]] + got
            else:

                @pl.when(owns_off if tag[0] == "t" else owns_diag)
                def _():
                    hop(tag, i).wait_recv()
                    both = acc[0] + at(tag + "r%d" % i)[...].astype(F32)
                    if tag[0] == "d":
                        piece[...] = both
                    elif tag[0] == "t":
                        piece[pl.ds((n - 1) * group, r), :] += both
                    else:
                        at(tag + "sx")[...] = both.astype(BF16)
                        ucopy(tag).start()
        if n == 0:
            hop("h", i).wait_recv()
            both = at("hs%d" % i)[...] + at("hr%d" % i)[...]
            if i < stages:
                at("hs%d" % (i + 1))[...] = both
            else:
                rhs[...] = both

    def place(n):
        tag = "u%d" % (n - 1)

        @pl.when(owns_off)
        def _():
            ucopy(tag).wait_recv()
            got = at(tag + "rx")[...]
            spots = [n - 1] if n - 1 < full else [full, full + 1]
            for g in spots:
                columns = hot[:, pl.ds(g * LANES, LANES)]
                piece[...] += lax.dot_general(
                    got, columns, (((1,), (1,)), ((), ())), preferred_element_type=F32
                )

    count = len(items)
    done = [-1] * count

    def advance(n):
        step = done[n] + 1
        if step == 0:
            produce(n)
            push(n, 0)
        elif step <= stages + 1:
            pull(n, step - 1)
            if step <= stages:
                push(n, step)
        elif step == stages + 2 and n > 0:
            place(n)
        else:
            return
        done[n] = step

    for n in range(count):
        for m in range(n):
            advance(m)
        advance(n)
        for m in range(n):
            advance(m)
    for _ in range(stages + 2):
        for m in range(count):
            advance(m)

    for c in range(full + 1):
        xcopy(c).wait_send()
    for item in items:
        for tag, r, w in item:
            for i in range(stages):
                hop(tag, i).wait_send()

            @pl.when(owns_diag if tag[0] == "t" else owns_off)
            def _():
                hop(tag, stages).wait_send()

            if tag[0] == "u":

                @pl.when(owns_diag)
                def _():
                    ucopy(tag).wait_send()

    for i in range(stages + 1):
        hop("h", i).wait_send()


def shards(panels, pattern, point_inverse, camera_hessian, damping, camera_grad, point_grad):
    nk, rows, width = panels.shape
    slabs = lax.axis_size("pair") // lax.axis_size("blk")
    own = width // slabs
    group = LANES // slabs
    names, items, stages, full, rest = plan(nk, rows, width, slabs, own, group)
    hot = jnp.asarray(column_order(width, slabs, group), BF16)
    vmem = pl.BlockSpec(memory_space=pltpu.VMEM)
    piece, rhs = pl.pallas_call(
        functools.partial(kernel, names, items, stages, full, rest, slabs, group),
        out_shape=(
            jax.ShapeDtypeStruct((own, width), F32),
            jax.ShapeDtypeStruct((8, width), F32),
        ),
        in_specs=[pl.BlockSpec(memory_space=pltpu.SMEM)] + [vmem] * 4,
        out_specs=(vmem, vmem),
        scratch_shapes=names.shapes,
        compiler_params=pltpu.CompilerParams(
            collective_id=0, has_side_effects=True, vmem_limit_bytes=50 * 2**20
        ),
    )(pattern, panels, point_inverse, point_grad, hot)
    return finish(piece, rhs[0], camera_hessian, damping, camera_grad, own)


def fits(mesh):
    pairs = mesh.shape["pair"]
    return mesh.shape["blk"] == 2 and pairs & (pairs - 1) == 0 and 4 <= pairs <= 32


def solution(mesh):
    def program(panels, pattern, point_inverse, camera_hessian, damping, camera_grad, point_grad):
        use = fits(mesh)
        if use:
            slabs = mesh.shape["pair"] // 2
            width = camera_hessian.shape[1]
            own, group = width // slabs, LANES // slabs
            use = (
                width % slabs == 0
                and own % 8 == 0
                and group % 8 == 0
                and own % group * slabs * 2 == LANES
                and panels.shape[0] // mesh.shape["pair"] % 2 == 0
                and point_inverse.shape[2] == LANES
            )
        return jax.shard_map(
            shards if use else general_shards,
            mesh=mesh,
            in_specs=(
                P("pair", None, "blk"),
                P("pair", "blk"),
                P("pair", None, None),
                P("blk", None),
                P("blk"),
                P("blk"),
                P("pair", None),
            ),
            out_specs=(P("pair", "blk"), P("blk")),
            check_vma=False,
        )(panels, pattern, point_inverse, camera_hessian, damping, camera_grad, point_grad)

    return program
```

time: 182 us -> 78.4 us (0.43)
  waiting for transfers between devices: 90.7 us -> 0 us
  Pallas kernels: 0 us -> 68.2 us
  blocking collectives: 33.6 us -> 0 us
  local copies, waits for them, and re-layouts: 19.8 us -> 5.99 us
  between operations: 14.1 us -> 0.75 us
  matrix products: 11.9 us -> 0 us
  other arithmetic: 11.1 us -> 2.33 us
    all_gather x1 -> x0, waiting for transfers between devices: 68.4 us -> none  [shards(): gathered = lax.all_gather(scaled, 'blk', axis=1, tiled=True)]
    pallas_call x0 -> x1, Pallas kernels: none -> 68.2 us  [shards(): pl.pallas_call(functools.partial(kernel, names, items, stages, full, rest...]
    psum x1 -> x0, blocking collectives: 33.6 us -> none  [shards(): summed = lax.psum(local_terms, 'pair')]
    unnamed x3 -> x0, waiting for transfers between devices: 22.3 us -> none
    dot_general x2 -> x0, matrix products: 11.9 us -> none  [the longest x1 9.4 us: shards(): lax.dot_general(gathered, flat_panels, (((0,), (0,)), ((), ())), preferre...]
    another operation x4 -> x0, other arithmetic: 6.04 us -> none
    gather x1 -> x0, local copies, waits for them, and re-layouts: 4.93 us -> none  [shards(): diag_vals = jnp.diagonal(camera_hessian)]
    unnamed x10 -> x13, local copies, waits for them, and re-layouts: 1.27 us -> 5.98 us
  transfers between devices with their start and end apart: 2 -> 0, of which waited for: 2 -> 0; matrix products, arithmetic and copies ran while one was open for 7% -> 0% of each run, Pallas kernels for 0% -> 0%
where the time goes in v1:
time: 78.4 us; the launch traced here: 77.3 us
  Pallas kernels  68.2 us (87%)
  local copies, waits for them, and re-layouts  5.99 us (8%)
  other arithmetic  2.33 us (3%)
    pallas_call x1, Pallas kernels, shards(): pl.pallas_call(functools.partial(kernel, names, items, stages, full, rest...  68.2 us
    unnamed x13, local copies, waits for them, and re-layouts  5.98 us
    sub x1, other arithmetic, finish(): schur = jnp.where(inside, damped, 0.0) - piece  1.72 us

profile of v1, /device:TPU:0, one launch (start us, length us, event | category | flops | bytes accessed | tf_op | source)
XLA Modules:
  0.0 77.3 jit_solution(8549465631907283115)
XLA Ops:
  0.6 0.7 copy.10.pattern
  1.4 0.0 copy-start.2
  1.4 0.0 copy-start.1
  1.4 4.0 %copy.11.panels = bf16[6,384,576]{2,1,0:T(8,128)(2,1)S(1)} copy(bf16[6,384,576]{1,2,0:T(8,128)(2,1)} %param.8) | data formatting | bytes 5308416 | tf_op args[0]
  5.4 0.0 copy-done.2
  5.4 0.0 copy-start.4
  5.4 0.0 copy-start.3
  5.5 0.0 copy-done.1
  5.5 0.0 copy-start
  5.5 1.2 %copy-done = bf16[576,768]{1,0:T(8,128)(2,1)S(1)} copy-done((bf16[576,768]{1,0:T(8,128)(2,1)S(1)}, bf16[576,768]{1,0:T(8,128)(2,1)}, u32[]{:S(2)}) %copy-start) | copy-done | bytes 884760
  6.7 68.2 %shard_map.95 = (f32[72,576]{1,0:T(8,128)S(1)}, f32[8,576]{1,0:T(8,128)S(1)}) custom-call(s32[6,1]{1,0:T(8,128)S(1)} %copy.10.pattern, bf16[6,384,576]{2,1,0:T(8,128)(2,1)S(1)} %copy.11.panels, f32[6,9,128]{2,1,0:T(8,128)S(1)} %copy.12.inverse, f32[6,384]{1,0:T(8,128)S(1)} %copy-done.1, bf16[576,768]{1,0:T(8,128)(2,1)S(1)} %copy-done), custom_call_target="tpu_custom_call" | custom-call | tf_op jit(solution)/shard_map/pallas_call | solution.py:377
  74.9 0.0 copy-done.4
  75.0 1.7 %select_subtract_fusion = f32[72,576]{1,0:T(8,128)} fusion(f32[72,576]{1,0:T(8,128)S(1)} %get-tuple-element.4, f32[576,576]{1,0:T(8,128)} %param.11, s32[]{:T(128)S(6)} %min.4, f32[576]{0:T(1024)S(1)} %convert_multiply_fusion, s32[72]{0:T(128)S(1)} %iota_add_fusion, pred[]{:T(512)S(6)} %and.5), kind=kLoop, calls=%fused_computation | loop fusion | flops 248832 | bytes 500261 | tf_op jit(solution)/shard_map/sub | solution.py:38
  76.7 0.0 copy-done.3
  76.7 0.6 sub.11
  (4 shorter events, 0.0 us)
Async XLA Ops:
  1.4 4.1 %copy-start.2 = (f32[6,9,128]{2,0,1:T(8,128)S(1)}, f32[6,9,128]{2,0,1:T(8,128)}, u32[]{:S(2)}) copy-start(f32[6,9,128]{2,0,1:T(8,128)} %param.10) | copy-start | bytes 82948
  1.4 4.1 %copy-start.1 = (f32[6,384]{1,0:T(8,128)S(1)}, f32[6,384]{1,0:T(8,128)}, u32[]{:S(2)}) copy-start(f32[6,384]{1,0:T(8,128)} %grads.1) | copy-start | bytes 27652
  5.4 69.5 %copy-start.4 = (s32[576]{0:T(1024)S(1)}, s32[576]{0:T(1024)}, u32[]{:S(2)}) copy-start(s32[576]{0:T(1024)} %param.12) | copy-start | bytes 6916
  5.4 71.3 %copy-start.3 = (f32[576]{0:T(1024)S(1)}, f32[576]{0:T(1024)}, u32[]{:S(2)}) copy-start(f32[576]{0:T(1024)} %param.13) | copy-start | bytes 6916
  5.5 1.2 %copy-start = (bf16[576,768]{1,0:T(8,128)(2,1)S(1)}, bf16[576,768]{1,0:T(8,128)(2,1)}, u32[]{:S(2)}) copy-start(bf16[576,768]{1,0:T(8,128)(2,1)} %constant.26.clone.hot) | copy-start | bytes 2654212

commit v2 on v1

--- a/solution.py
+++ b/solution.py
@@ -2,7 +2,6 @@
 
 import jax
 import jax.numpy as jnp
-import numpy as np
 from jax import lax
 from jax.experimental import pallas as pl
 from jax.experimental.pallas import tpu as pltpu
@@ -64,22 +63,6 @@
     return finish(piece, summed, camera_hessian, damping, camera_grad, own_rows)
 
 
-def column_order(width, slabs, group):
-    own = width // slabs
-    full, rest = own // group, own % group
-    hot = np.zeros((width, (full + 2) * LANES), np.float32)
-    for c in range(full):
-        for s in range(slabs):
-            for r in range(group):
-                hot[s * own + c * group + r, c * LANES + s * group + r] = 1
-    for s in range(slabs):
-        for r in range(rest):
-            at = s * own + full * group + r
-            hot[at, full * LANES + s * rest + r] = 1
-            hot[at, (full + 1) * LANES + slabs * rest + s * rest + r] = 1
-    return hot
-
-
 class Names:
     def __init__(self):
         self.order, self.shapes = {}, []
@@ -89,20 +72,20 @@
         self.shapes.append(shape)
 
 
-def tdot(a, b):
-    return lax.dot_general(a, b, (((0,), (0,)), ((), ())), preferred_element_type=F32)
+def ndot(a, b):
+    return lax.dot_general(a, b, (((1,), (1,)), ((), ())), preferred_element_type=F32)
 
 
 def plan(nk, rows, width, slabs, own, group):
-    full, rest = own // group, own % group
+    sizes = [group] * (own // group)
+    if own % group:
+        sizes.append(own % group)
     stages = slabs.bit_length() - 1
     half = nk // 2 * rows
     names = Names()
     items = [[("d", own, width)]]
-    for c in range(full):
-        items.append([("t%d" % c, group, width), ("u%d" % c, own, LANES)])
-    items.append([("t%d" % full, rest, width), ("u%d" % full, own, LANES)])
-    copies = 0
+    for c, g in enumerate(sizes):
+        items.append([("t%d" % c, g, width), ("u%d" % c, own, slabs * g)])
     for item in items:
         for tag, r, w in item:
             n = slabs
@@ -120,25 +103,27 @@
     for i in range(stages + 1):
         names.add("hs%d" % i, pltpu.VMEM((8, width), F32))
         names.add("hr%d" % i, pltpu.VMEM((8, width), F32))
-    for c in range(full + 1):
-        deep = half if c < full else half // 2
-        names.add("xs%d" % c, pltpu.VMEM((deep, LANES), BF16))
-        names.add("xr%d" % c, pltpu.VMEM((deep, LANES), BF16))
-    names.add("scaled", pltpu.VMEM((nk, rows, width), BF16))
-    names.add("mine", pltpu.VMEM((half, width), BF16))
-    names.add("total", pltpu.VMEM((width, width), F32))
+    for c, g in enumerate(sizes):
+        names.add("xs%d" % c, pltpu.VMEM((slabs * g, half), BF16))
+        names.add("xr%d" % c, pltpu.VMEM((slabs * g, half), BF16))
+        names.add("hot%d" % c, pltpu.VMEM((width, slabs * g), BF16))
+    names.add("raw", pltpu.VMEM((nk, width, rows), BF16))
+    names.add("scaled", pltpu.VMEM((2, width, half), BF16))
+    names.add("masked", pltpu.VMEM((2, width, half), BF16))
     count = len(names.shapes)
     names.add("send", pltpu.SemaphoreType.DMA((count,)))
     names.add("recv", pltpu.SemaphoreType.DMA((count,)))
-    return names, items, stages, full, rest
-
-
-def kernel(names, items, stages, full, rest, slabs, group, pattern, panels, inverse, grads, hot, piece, rhs, *refs):
+    names.add("load", pltpu.SemaphoreType.DMA((nk,)))
+    return names, items, stages, sizes
+
+
+def kernel(names, items, stages, sizes, slabs, group, pattern, panels, inverse, grads, piece, rhs, *refs):
     at = lambda name: refs[names.order[name]]
-    nk, rows, width = panels.shape
+    nk, width, rows = panels.shape
     points = rows // 3
     half = nk // 2 * rows
     own = width // slabs
+    last = len(sizes) - 1
     blk = lax.axis_index("blk")
     pair = lax.axis_index("pair")
     bit = [lax.rem(lax.div(pair, 2**i), 2) for i in range(stages + 1)]
@@ -147,6 +132,15 @@
     top = bit[stages]
     owns_diag = top == blk
     owns_off = top != blk
+    first = blk * (nk // 2)
+    other_first = (1 - blk) * (nk // 2)
+    order = [first + j for j in range(nk // 2)] + [other_first + j for j in range(nk // 2)]
+
+    def load(m):
+        return pltpu.make_async_copy(panels.at[order[m]], at("raw").at[order[m]], at("load").at[m])
+
+    for m in range(nk):
+        load(m).start()
 
     barrier = pltpu.get_barrier_semaphore()
     for other in mate + [across]:
@@ -172,89 +166,73 @@
     def ucopy(tag):
         return copy(tag + "sx", tag + "rx", across)
 
-    first = blk * (nk // 2)
-    other_first = (1 - blk) * (nk // 2)
-    for j in range(nk // 2):
-        seen = pattern[first + j, 0].astype(F32)
-        at("mine")[pl.ds(j * rows, rows), :] = (panels[first + j].astype(F32) * seen).astype(BF16)
-
-    def fill(c):
-        if c < full:
-            columns = hot[:, pl.ds(c * LANES, LANES)]
-            at("xs%d" % c)[...] = jnp.dot(at("mine")[...], columns, preferred_element_type=F32).astype(BF16)
-        else:
-            low = hot[:, pl.ds(full * LANES, LANES)]
-            high = hot[:, pl.ds((full + 1) * LANES, LANES)]
-            upper = at("mine")[pl.ds(0, half // 2), :]
-            lower = at("mine")[pl.ds(half // 2, half // 2), :]
-            packed = jnp.dot(upper, low, preferred_element_type=F32)
-            packed = packed + jnp.dot(lower, high, preferred_element_type=F32)
-            at("xs%d" % c)[...] = packed.astype(BF16)
-
-    fill(0)
+    def pick(values, k):
+        chosen = lax.broadcasted_iota(jnp.int32, values.shape, 0) == k
+        return jnp.sum(jnp.where(chosen, values, 0.0), axis=0, keepdims=True)
+
+    def observe(m):
+        load(m).wait()
+        k = order[m]
+        wide = at("raw")[k].astype(F32) * pattern[0, k].astype(F32)
+        lanes = pl.ds(m % (nk // 2) * rows, rows)
+        at("masked")[m // (nk // 2), :, lanes] = wide.astype(BF16)
+        if m < nk // 2:
+            start = 0
+            for c, g in enumerate(sizes):
+                parts = [wide[s * own + start : s * own + start + g] for s in range(slabs)]
+                at("xs%d" % c)[:, lanes] = jnp.concatenate(parts, axis=0).astype(BF16)
+                start += g
+
+    for m in range(nk // 2):
+        observe(m)
     pl.semaphore_wait(barrier, len(mate) + 1)
-    xcopy(0).start()
-    for c in range(1, full + 1):
-        fill(c)
-        if c == 1:
-            xcopy(c).start()
-
-    at("total")[...] = jnp.zeros((width, width), F32)
-    at("hs0")[...] = jnp.zeros((8, width), F32)
+    for c in range(min(3, len(sizes))):
+        xcopy(c).start()
+    for m in range(nk // 2, nk):
+        observe(m)
+
     piece[...] = jnp.zeros_like(piece)
-
-    def block(k, carry):
-        seen = pattern[k, 0].astype(F32)
-        masked = (panels[k].astype(F32) * seen).astype(BF16)
-        wide = masked.astype(F32)
-        flat = inverse[k]
-        tall = jnp.concatenate([flat, jnp.zeros((16 - 9, points), F32)], axis=0).T
-        picked = lax.broadcasted_iota(jnp.int32, grads.shape, 0) == k
-        grad = jnp.sum(jnp.where(picked, grads[...], 0.0), axis=0, keepdims=True)
-        parts, steps = [], []
+    flat = [inverse[n] for n in range(9)]
+    terms = jnp.zeros((8, width), F32)
+    for m in range(nk):
+        side, lanes = m // (nk // 2), m % (nk // 2) * rows
+        k = order[m]
+        near = [pick(flat[n], k) for n in range(9)]
+        grad = pick(grads[...], k)
+        wide = [at("masked")[side, :, pl.ds(lanes + c * points, points)].astype(F32) for c in range(3)]
+        steps = []
         for a in range(3):
             total, step = None, None
             for c in range(3):
-                n = a * 3 + c
-                term = tall[:, n : n + 1] * wide[c * points : (c + 1) * points]
-                part = flat[n : n + 1] * grad[:, c * points : (c + 1) * points]
+                term = near[a * 3 + c] * wide[c]
+                part = near[a * 3 + c] * grad[:, c * points : (c + 1) * points]
                 total = term if total is None else total + term
                 step = part if step is None else step + part
-            parts.append(total.astype(BF16))
+            at("scaled")[side, :, pl.ds(lanes + a * points, points)] = total.astype(BF16)
             steps.append(step)
-        for a in range(3):
-            at("scaled")[k, pl.ds(a * points, points), :] = parts[a]
-        at("total")[...] += tdot(at("scaled")[k], masked)
         stepped = jnp.broadcast_to(jnp.concatenate(steps, axis=1), (8, rows)).astype(BF16)
-        at("hs0")[...] += jnp.dot(stepped, masked, preferred_element_type=F32)
-        return carry
-
-    lax.fori_loop(0, nk, block, 0)
-
-    def held():
-        return at("scaled")[pl.ds(other_first, nk // 2)].reshape(half, width)
+        terms = terms + ndot(stepped, at("masked")[side, :, pl.ds(lanes, rows)])
+    at("hs0")[...] = terms
 
     def produce(n):
         if n == 0:
-            at("da0")[...] = at("total")[...].reshape(slabs, own, width)
+            total = ndot(at("scaled")[0], at("masked")[0])
+            total = total + ndot(at("scaled")[1], at("masked")[1])
+            at("da0")[...] = total.reshape(slabs, own, width)
             return
-        c = n - 1
+        c, g = n - 1, sizes[n - 1]
         xcopy(c).wait_recv()
-        if c + 2 <= full:
-            xcopy(c + 2).start()
+        if c + 3 <= last:
+            xcopy(c + 3).start()
         got = at("xr%d" % c)[...]
-        mix = held()
-        if c < full:
-            at("t%da0" % c)[...] = tdot(got, mix).reshape(slabs, group, width)
-            at("u%da0" % c)[...] = tdot(mix, got).reshape(slabs, own, LANES)
-        else:
-            packed = slabs * rest
-            upper, lower = mix[: half // 2], mix[half // 2 :]
-            both = tdot(got, upper)[:packed] + tdot(got, lower)[packed : 2 * packed]
-            at("t%da0" % c)[...] = both.reshape(slabs, rest, width)
-            lane = lax.broadcasted_iota(jnp.int32, (width, LANES), 1)
-            side = jnp.where(lane < packed, tdot(upper, got), tdot(lower, got))
-            at("u%da0" % c)[...] = side.reshape(slabs, own, LANES)
+        mix = at("scaled")[1]
+        at("t%da0" % c)[...] = ndot(got, mix).reshape(slabs, g, width)
+        at("u%da0" % c)[...] = ndot(mix, got).reshape(slabs, own, slabs * g)
+        row = lax.broadcasted_iota(jnp.int32, (width, slabs * g), 0)
+        lane = lax.broadcasted_iota(jnp.int32, (width, slabs * g), 1)
+        shift = g.bit_length() - 1
+        goal = lax.shift_right_logical(lane, shift) * own + c * group + (lane & (g - 1))
+        at("hot%d" % c)[...] = jnp.where(row == goal, 1.0, 0.0).astype(BF16)
 
     def push(n, i):
         for tag, r, w in items[n]:
@@ -310,12 +288,7 @@
         def _():
             ucopy(tag).wait_recv()
             got = at(tag + "rx")[...]
-            spots = [n - 1] if n - 1 < full else [full, full + 1]
-            for g in spots:
-                columns = hot[:, pl.ds(g * LANES, LANES)]
-                piece[...] += lax.dot_general(
-                    got, columns, (((1,), (1,)), ((), ())), preferred_element_type=F32
-                )
+            piece[...] += ndot(got, at("hot%d" % (n - 1))[...])
 
     count = len(items)
     done = [-1] * count
@@ -345,7 +318,7 @@
         for m in range(count):
             advance(m)
 
-    for c in range(full + 1):
+    for c in range(last + 1):
         xcopy(c).wait_send()
     for item in items:
         for tag, r, w in item:
@@ -371,22 +344,26 @@
     slabs = lax.axis_size("pair") // lax.axis_size("blk")
     own = width // slabs
     group = LANES // slabs
-    names, items, stages, full, rest = plan(nk, rows, width, slabs, own, group)
-    hot = jnp.asarray(column_order(width, slabs, group), BF16)
+    names, items, stages, sizes = plan(nk, rows, width, slabs, own, group)
     vmem = pl.BlockSpec(memory_space=pltpu.VMEM)
     piece, rhs = pl.pallas_call(
-        functools.partial(kernel, names, items, stages, full, rest, slabs, group),
+        functools.partial(kernel, names, items, stages, sizes, slabs, group),
         out_shape=(
             jax.ShapeDtypeStruct((own, width), F32),
             jax.ShapeDtypeStruct((8, width), F32),
         ),
-        in_specs=[pl.BlockSpec(memory_space=pltpu.SMEM)] + [vmem] * 4,
+        in_specs=[
+            pl.BlockSpec(memory_space=pltpu.SMEM),
+            pl.BlockSpec(memory_space=pl.ANY),
+            vmem,
+            vmem,
+        ],
         out_specs=(vmem, vmem),
         scratch_shapes=names.shapes,
         compiler_params=pltpu.CompilerParams(
-            collective_id=0, has_side_effects=True, vmem_limit_bytes=50 * 2**20
+            collective_id=0, has_side_effects=True, vmem_limit_bytes=56 * 2**20
         ),
-    )(pattern, panels, point_inverse, point_grad, hot)
+    )(pattern.T, jnp.swapaxes(panels, 1, 2), jnp.swapaxes(point_inverse, 0, 1), point_grad)
     return finish(piece, rhs[0], camera_hessian, damping, camera_grad, own)
 
 

time: 78.4 us -> 70.3 us (0.90)
  local copies, waits for them, and re-layouts: 5.99 us -> 0.74 us
  Pallas kernels: 68.2 us -> 64.4 us
    unnamed x13 -> x2, local copies, waits for them, and re-layouts: 5.98 us -> 0.01 us
    pallas_call x1, Pallas kernels: 68.2 us -> 64.4 us  [shards(): pl.pallas_call(functools.partial(kernel, names, items, stages, sizes, sla...]
where the time goes in v2:
time: 70.3 us; the launch traced here: 68.9 us
  Pallas kernels  64.4 us (92%)
  other arithmetic  3.1 us (4%)
  local copies, waits for them, and re-layouts  0.74 us (1%)
    pallas_call x1, Pallas kernels, shards(): pl.pallas_call(functools.partial(kernel, names, items, stages, sizes, sla...  64.4 us
    sub x1, other arithmetic, finish(): schur = jnp.where(inside, damped, 0.0) - piece  1.81 us

profile of v2, /device:TPU:0, one launch (start us, length us, event | category | flops | bytes accessed | tf_op | source)
XLA Modules:
  0.0 68.9 jit_solution(9021260514637397912)
XLA Ops:
  0.7 0.7 %convert_multiply_fusion = f32[576]{0:T(1024)S(1)} fusion(s32[576]{0:T(1024)} %param.11), kind=kLoop, calls=%fused_computation.2 | loop fusion | flops 1728 | bytes 4608 | tf_op jit(solution)/shard_map/mul | solution.py:33
  1.3 0.0 copy-start
  1.4 64.4 %shard_map.86 = (f32[72,576]{1,0:T(8,128)}, f32[8,576]{1,0:T(8,128)}) custom-call(s32[1,6]{1,0:T(1,128)} %bitcast.5, bf16[6,576,384]{2,1,0:T(8,128)(2,1)} %bitcast.3, f32[9,6,128]{2,1,0:T(8,128)} %bitcast.4, f32[6,384]{1,0:T(8,128)} %grads.1), custom_call_target="tpu_custom_call" | custom-call | tf_op jit(solution)/shard_map/pallas_call | solution.py:349
  65.8 1.8 %select_subtract_fusion = f32[72,576]{1,0:T(8,128)} fusion(f32[72,576]{1,0:T(8,128)} %get-tuple-element.4, f32[576,576]{1,0:T(8,128)} %param.10, s32[]{:T(128)S(6)} %min.4, f32[576]{0:T(1024)S(1)} %convert_multiply_fusion, s32[72]{0:T(128)S(1)} %iota_add_fusion, pred[]{:T(512)S(6)} %and.5), kind=kLoop, calls=%fused_computation | loop fusion | flops 248832 | bytes 500261 | tf_op jit(solution)/shard_map/sub | solution.py:37
  67.6 0.7 %slice_reduce_fusion = f32[576]{0:T(1024)S(1)} fusion(f32[8,576]{1,0:T(8,128)} %get-tuple-element.5), kind=kLoop, calls=%fused_computation.3 | loop fusion | bytes 4608 | tf_op jit(solution)/shard_map/slice | solution.py:367
  68.3 0.0 copy-done
  68.3 0.6 sub.11
  (1 shorter events, 0.0 us)
Async XLA Ops:
  1.3 67.0 %copy-start = (f32[576]{0:T(1024)S(1)}, f32[576]{0:T(1024)}, u32[]{:S(2)}) copy-start(f32[576]{0:T(1024)} %param.12) | copy-start | bytes 6916

commit v3 on v2

--- a/solution.py
+++ b/solution.py
@@ -90,13 +90,19 @@
         for tag, r, w in item:
             n = slabs
             names.add(tag + "a0", pltpu.VMEM((n, r, w), F32))
-            for i in range(stages):
+            for i in range(stages if tag == "d" else 1):
                 n //= 2
                 names.add(tag + "s%d" % i, pltpu.VMEM((n * r, w), BF16))
                 names.add(tag + "r%d" % i, pltpu.VMEM((n * r, w), BF16))
                 names.add(tag + "a%d" % (i + 1), pltpu.VMEM((n, r, w), F32))
-            names.add(tag + "s%d" % stages, pltpu.VMEM((r, w), BF16))
-            names.add(tag + "r%d" % stages, pltpu.VMEM((r, w), BF16))
+            if tag == "d":
+                names.add(tag + "s%d" % stages, pltpu.VMEM((r, w), BF16))
+                names.add(tag + "r%d" % stages, pltpu.VMEM((r, w), BF16))
+            else:
+                names.add(tag + "out", pltpu.VMEM((slabs // 2, r, w), BF16))
+                names.add(tag + "in", pltpu.VMEM((slabs, r, w), BF16))
+                names.add(tag + "send", pltpu.SemaphoreType.DMA((slabs // 2,)))
+                names.add(tag + "recv", pltpu.SemaphoreType.DMA((slabs,)))
             if tag[0] == "u":
                 names.add(tag + "sx", pltpu.VMEM((r, w), BF16))
                 names.add(tag + "rx", pltpu.VMEM((r, w), BF16))
@@ -143,7 +149,11 @@
         load(m).start()
 
     barrier = pltpu.get_barrier_semaphore()
-    for other in mate + [across]:
+    place_here = lax.div(pair, 2)
+    for step in range(1, slabs):
+        peer = {"pair": lax.rem(place_here + step, slabs) * 2 + bit[0]}
+        pl.semaphore_signal(barrier, inc=1, device_id=peer, device_id_type=MESH)
+    for other in [mate[0], across]:
         pl.semaphore_signal(barrier, inc=1, device_id=other, device_id_type=MESH)
 
     def copy(src, dst, other):
@@ -162,6 +172,30 @@
 
     def hop(tag, i):
         return copy(tag + "s%d" % i, tag + "r%d" % i, mate[i])
+
+    def owner(tag, q):
+        side = 1 - blk if tag[0] == "t" else blk
+        return side * slabs + q * 2 + bit[0]
+
+    def direct(tag, q):
+        return pltpu.make_async_remote_copy(
+            src_ref=at(tag + "out").at[q],
+            dst_ref=at(tag + "in").at[place_here],
+            send_sem=at(tag + "send").at[q],
+            recv_sem=at(tag + "recv").at[place_here],
+            device_id={"pair": owner(tag, q)},
+            device_id_type=MESH,
+        )
+
+    def arrival(tag, j):
+        return pltpu.make_async_remote_copy(
+            src_ref=at(tag + "out").at[0],
+            dst_ref=at(tag + "in").at[j],
+            send_sem=at(tag + "send").at[0],
+            recv_sem=at(tag + "recv").at[j],
+            device_id=mate[0],
+            device_id_type=MESH,
+        )
 
     def ucopy(tag):
         return copy(tag + "sx", tag + "rx", across)
@@ -185,7 +219,7 @@
 
     for m in range(nk // 2):
         observe(m)
-    pl.semaphore_wait(barrier, len(mate) + 1)
+    pl.semaphore_wait(barrier, slabs + 1)
     for c in range(min(3, len(sizes))):
         xcopy(c).start()
     for m in range(nk // 2, nk):
@@ -239,14 +273,13 @@
             acc = at(tag + "a%d" % i)
             if i < stages:
                 count = slabs >> (i + 1)
-                cast = [acc[2 * m + 1 - bit[i]].astype(BF16) for m in range(count)]
                 for m in range(count):
-                    at(tag + "s%d" % i)[pl.ds(m * r, r), :] = cast[m]
+                    at(tag + "s%d" % i)[pl.ds(m * r, r), :] = acc[2 * m + 1 - bit[i]].astype(BF16)
                 hop(tag, i).start()
             else:
                 at(tag + "s%d" % i)[...] = acc[0].astype(BF16)
 
-                @pl.when(owns_diag if tag[0] == "t" else owns_off)
+                @pl.when(owns_off)
                 def _():
                     hop(tag, i).start()
         if n == 0:
@@ -262,17 +295,10 @@
                     at(tag + "a%d" % (i + 1))[m] = acc[2 * m + bit[i]] + got
             else:
 
-                @pl.when(owns_off if tag[0] == "t" else owns_diag)
+                @pl.when(owns_diag)
                 def _():
                     hop(tag, i).wait_recv()
-                    both = acc[0] + at(tag + "r%d" % i)[...].astype(F32)
-                    if tag[0] == "d":
-                        piece[...] = both
-                    elif tag[0] == "t":
-                        piece[pl.ds((n - 1) * group, r), :] += both
-                    else:
-                        at(tag + "sx")[...] = both.astype(BF16)
-                        ucopy(tag).start()
+                    piece[...] = acc[0] + at(tag + "r%d" % i)[...].astype(F32)
         if n == 0:
             hop("h", i).wait_recv()
             both = at("hs%d" % i)[...] + at("hr%d" % i)[...]
@@ -281,6 +307,41 @@
             else:
                 rhs[...] = both
 
+    def scatter(n):
+        for tag, r, w in items[n]:
+            for q in range(slabs // 2):
+                cast = at(tag + "a1")[q].astype(BF16)
+                at(tag + "out")[q] = cast
+                here = owner(tag, q) == pair
+
+                @pl.when(here)
+                def _():
+                    at(tag + "in")[place_here] = cast
+
+                @pl.when(jnp.logical_not(here))
+                def _():
+                    direct(tag, q).start()
+
+    def collect(n):
+        for tag, r, w in items[n]:
+
+            @pl.when(owns_off if tag[0] == "t" else owns_diag)
+            def _():
+                for j in range(slabs):
+
+                    @pl.when(place_here != j)
+                    def _():
+                        arrival(tag, j).wait_recv()
+
+                total = at(tag + "in")[0].astype(F32)
+                for j in range(1, slabs):
+                    total = total + at(tag + "in")[j].astype(F32)
+                if tag[0] == "t":
+                    piece[pl.ds((n - 1) * group, r), :] += total
+                else:
+                    at(tag + "sx")[...] = total.astype(BF16)
+                    ucopy(tag).start()
+
     def place(n):
         tag = "u%d" % (n - 1)
 
@@ -298,36 +359,47 @@
         if step == 0:
             produce(n)
             push(n, 0)
-        elif step <= stages + 1:
+        elif n == 0 and step <= stages + 1:
             pull(n, step - 1)
             if step <= stages:
                 push(n, step)
-        elif step == stages + 2 and n > 0:
+        elif n > 0 and step == 1:
+            pull(n, 0)
+            scatter(n)
+        elif n > 0 and step == 2:
+            collect(n)
+        elif n > 0 and step == 3:
             place(n)
         else:
             return
         done[n] = step
 
     for n in range(count):
-        for m in range(n):
-            advance(m)
         advance(n)
         for m in range(n):
             advance(m)
-    for _ in range(stages + 2):
+    for _ in range(3):
         for m in range(count):
             advance(m)
+    assert done == [stages + 1] + [3] * (count - 1)
 
     for c in range(last + 1):
         xcopy(c).wait_send()
     for item in items:
         for tag, r, w in item:
-            for i in range(stages):
+            for i in range(stages if tag == "d" else 1):
                 hop(tag, i).wait_send()
-
-            @pl.when(owns_diag if tag[0] == "t" else owns_off)
-            def _():
-                hop(tag, stages).wait_send()
+            if tag == "d":
+
+                @pl.when(owns_off)
+                def _():
+                    hop(tag, stages).wait_send()
+            else:
+                for q in range(slabs // 2):
+
+                    @pl.when(owner(tag, q) != pair)
+                    def _():
+                        direct(tag, q).wait_send()
 
             if tag[0] == "u":
 

time: 70.3 us -> 62.1 us (0.88); the launches traced: 68.9 us -> 61.8 us
  Pallas kernels: 64.4 us -> 57.3 us
    pallas_call x1, Pallas kernels: 64.4 us -> 57.3 us  [shards(): pl.pallas_call(functools.partial(kernel, names, items, stages, sizes, sla...]
where the time goes in v3:
time: 62.1 us; the launch traced here: 61.8 us
  Pallas kernels  57.3 us (92%)
  other arithmetic  3.1 us (5%)
  local copies, waits for them, and re-layouts  0.74 us (1%)
  between operations  0.67 us (1%)
    pallas_call x1, Pallas kernels, shards(): pl.pallas_call(functools.partial(kernel, names, items, stages, sizes, sla...  57.3 us
    sub x1, other arithmetic, finish(): schur = jnp.where(inside, damped, 0.0) - piece  1.81 us

profile of v3, /device:TPU:0, one launch (start us, length us, event | category | flops | bytes accessed | tf_op | source)
XLA Modules:
  0.0 61.8 jit_solution(448417807375795277)
XLA Ops:
  0.7 0.7 %convert_multiply_fusion = f32[576]{0:T(1024)S(1)} fusion(s32[576]{0:T(1024)} %param.11), kind=kLoop, calls=%fused_computation.2 | loop fusion | flops 1728 | bytes 4608 | tf_op jit(solution)/shard_map/mul | solution.py:33
  1.3 0.0 copy-start
  1.4 57.3 %shard_map.86 = (f32[72,576]{1,0:T(8,128)}, f32[8,576]{1,0:T(8,128)}) custom-call(s32[1,6]{1,0:T(1,128)} %bitcast.5, bf16[6,576,384]{2,1,0:T(8,128)(2,1)} %bitcast.3, f32[9,6,128]{2,1,0:T(8,128)} %bitcast.4, f32[6,384]{1,0:T(8,128)} %grads.1), custom_call_target="tpu_custom_call" | custom-call | tf_op jit(solution)/shard_map/pallas_call | solution.py:421
  58.6 1.8 %select_subtract_fusion = f32[72,576]{1,0:T(8,128)} fusion(f32[72,576]{1,0:T(8,128)} %get-tuple-element.4, f32[576,576]{1,0:T(8,128)} %param.10, s32[]{:T(128)S(6)} %min.4, f32[576]{0:T(1024)S(1)} %convert_multiply_fusion, s32[72]{0:T(128)S(1)} %iota_add_fusion, pred[]{:T(512)S(6)} %and.5), kind=kLoop, calls=%fused_computation | loop fusion | flops 248832 | bytes 500261 | tf_op jit(solution)/shard_map/sub | solution.py:37
  60.4 0.7 %slice_reduce_fusion = f32[576]{0:T(1024)S(1)} fusion(f32[8,576]{1,0:T(8,128)} %get-tuple-element.5), kind=kLoop, calls=%fused_computation.3 | loop fusion | bytes 4608 | tf_op jit(solution)/shard_map/slice | solution.py:439
  61.2 0.0 copy-done
  61.2 0.6 sub.11
  (1 shorter events, 0.0 us)
Async XLA Ops:
  1.3 59.8 %copy-start = (f32[576]{0:T(1024)S(1)}, f32[576]{0:T(1024)}, u32[]{:S(2)}) copy-start(f32[576]{0:T(1024)} %param.12) | copy-start | bytes 6916

commit v4 on v3

--- a/solution.py
+++ b/solution.py
@@ -260,13 +260,17 @@
             xcopy(c + 3).start()
         got = at("xr%d" % c)[...]
         mix = at("scaled")[1]
-        at("t%da0" % c)[...] = ndot(got, mix).reshape(slabs, g, width)
-        at("u%da0" % c)[...] = ndot(mix, got).reshape(slabs, own, slabs * g)
-        row = lax.broadcasted_iota(jnp.int32, (width, slabs * g), 0)
-        lane = lax.broadcasted_iota(jnp.int32, (width, slabs * g), 1)
-        shift = g.bit_length() - 1
-        goal = lax.shift_right_logical(lane, shift) * own + c * group + (lane & (g - 1))
-        at("hot%d" % c)[...] = jnp.where(row == goal, 1.0, 0.0).astype(BF16)
+        cross = ndot(mix, got)
+        at("u%da0" % c)[...] = cross.reshape(slabs, own, slabs * g)
+        at("t%da0" % c)[...] = cross.T.reshape(slabs, g, width)
+
+    def build_orders():
+        for c, g in enumerate(sizes):
+            row = lax.broadcasted_iota(jnp.int32, (width, slabs * g), 0)
+            lane = lax.broadcasted_iota(jnp.int32, (width, slabs * g), 1)
+            shift = g.bit_length() - 1
+            goal = lax.shift_right_logical(lane, shift) * own + c * group + (lane & (g - 1))
+            at("hot%d" % c)[...] = jnp.where(row == goal, 1.0, 0.0).astype(BF16)
 
     def push(n, i):
         for tag, r, w in items[n]:
@@ -359,6 +363,8 @@
         if step == 0:
             produce(n)
             push(n, 0)
+            if n == 0:
+                build_orders()
         elif n == 0 and step <= stages + 1:
             pull(n, step - 1)
             if step <= stages:

time: 62.1 us -> 62.5 us (level)
  no operation moved by 1% of the time
where the time goes in v4:
time: 62.5 us; the launch traced here: 62.1 us
  Pallas kernels  57.6 us (92%)
  other arithmetic  3.1 us (5%)
  local copies, waits for them, and re-layouts  0.74 us (1%)
  between operations  0.67 us (1%)
    pallas_call x1, Pallas kernels, shards(): pl.pallas_call(functools.partial(kernel, names, items, stages, sizes, sla...  57.6 us
    sub x1, other arithmetic, finish(): schur = jnp.where(inside, damped, 0.0) - piece  1.81 us

profile of v4, /device:TPU:0, one launch (start us, length us, event | category | flops | bytes accessed | tf_op | source)
XLA Modules:
  0.0 62.1 jit_solution(11316030849784985812)
XLA Ops:
  0.7 0.7 %convert_multiply_fusion = f32[576]{0:T(1024)S(1)} fusion(s32[576]{0:T(1024)} %param.11), kind=kLoop, calls=%fused_computation.2 | loop fusion | flops 1728 | bytes 4608 | tf_op jit(solution)/shard_map/mul | solution.py:33
  1.3 0.0 copy-start
  1.4 57.6 %shard_map.86 = (f32[72,576]{1,0:T(8,128)}, f32[8,576]{1,0:T(8,128)}) custom-call(s32[1,6]{1,0:T(1,128)} %bitcast.5, bf16[6,576,384]{2,1,0:T(8,128)(2,1)} %bitcast.3, f32[9,6,128]{2,1,0:T(8,128)} %bitcast.4, f32[6,384]{1,0:T(8,128)} %grads.1), custom_call_target="tpu_custom_call" | custom-call | tf_op jit(solution)/shard_map/pallas_call | solution.py:427
  59.0 1.8 %select_subtract_fusion = f32[72,576]{1,0:T(8,128)} fusion(f32[72,576]{1,0:T(8,128)} %get-tuple-element.4, f32[576,576]{1,0:T(8,128)} %param.10, s32[]{:T(128)S(6)} %min.4, f32[576]{0:T(1024)S(1)} %convert_multiply_fusion, s32[72]{0:T(128)S(1)} %iota_add_fusion, pred[]{:T(512)S(6)} %and.5), kind=kLoop, calls=%fused_computation | loop fusion | flops 248832 | bytes 500261 | tf_op jit(solution)/shard_map/sub | solution.py:37
  60.8 0.7 %slice_reduce_fusion = f32[576]{0:T(1024)S(1)} fusion(f32[8,576]{1,0:T(8,128)} %get-tuple-element.5), kind=kLoop, calls=%fused_computation.3 | loop fusion | bytes 4608 | tf_op jit(solution)/shard_map/slice | solution.py:445
  61.5 0.0 copy-done
  61.5 0.6 sub.11
  (1 shorter events, 0.0 us)
Async XLA Ops:
  1.3 60.2 %copy-start = (f32[576]{0:T(1024)S(1)}, f32[576]{0:T(1024)}, u32[]{:S(2)}) copy-start(f32[576]{0:T(1024)} %param.12) | copy-start | bytes 6916

commit v5 on v4

--- a/solution.py
+++ b/solution.py
@@ -220,7 +220,7 @@
     for m in range(nk // 2):
         observe(m)
     pl.semaphore_wait(barrier, slabs + 1)
-    for c in range(min(3, len(sizes))):
+    for c in range(min(2, len(sizes))):
         xcopy(c).start()
     for m in range(nk // 2, nk):
         observe(m)
@@ -256,8 +256,8 @@
             return
         c, g = n - 1, sizes[n - 1]
         xcopy(c).wait_recv()
-        if c + 3 <= last:
-            xcopy(c + 3).start()
+        if c + 2 <= last:
+            xcopy(c + 2).start()
         got = at("xr%d" % c)[...]
         mix = at("scaled")[1]
         cross = ndot(mix, got)

time: 62.5 us -> 62.5 us (level)
  no operation moved by 1% of the time
where the time goes in v5:
time: 62.5 us; the launch traced here: 62.1 us
  Pallas kernels  57.6 us (92%)
  other arithmetic  3.1 us (5%)
  local copies, waits for them, and re-layouts  0.74 us (1%)
  between operations  0.67 us (1%)
    pallas_call x1, Pallas kernels, shards(): pl.pallas_call(functools.partial(kernel, names, items, stages, sizes, sla...  57.6 us
    sub x1, other arithmetic, finish(): schur = jnp.where(inside, damped, 0.0) - piece  1.81 us

profile of v5, /device:TPU:0, one launch (start us, length us, event | category | flops | bytes accessed | tf_op | source)
XLA Modules:
  0.0 62.1 jit_solution(9522163875211984700)
XLA Ops:
  0.7 0.7 %convert_multiply_fusion = f32[576]{0:T(1024)S(1)} fusion(s32[576]{0:T(1024)} %param.11), kind=kLoop, calls=%fused_computation.2 | loop fusion | flops 1728 | bytes 4608 | tf_op jit(solution)/shard_map/mul | solution.py:33
  1.3 0.0 copy-start
  1.4 57.6 %shard_map.86 = (f32[72,576]{1,0:T(8,128)}, f32[8,576]{1,0:T(8,128)}) custom-call(s32[1,6]{1,0:T(1,128)} %bitcast.5, bf16[6,576,384]{2,1,0:T(8,128)(2,1)} %bitcast.3, f32[9,6,128]{2,1,0:T(8,128)} %bitcast.4, f32[6,384]{1,0:T(8,128)} %grads.1), custom_call_target="tpu_custom_call" | custom-call | tf_op jit(solution)/shard_map/pallas_call | solution.py:427
  59.0 1.8 %select_subtract_fusion = f32[72,576]{1,0:T(8,128)} fusion(f32[72,576]{1,0:T(8,128)} %get-tuple-element.4, f32[576,576]{1,0:T(8,128)} %param.10, s32[]{:T(128)S(6)} %min.4, f32[576]{0:T(1024)S(1)} %convert_multiply_fusion, s32[72]{0:T(128)S(1)} %iota_add_fusion, pred[]{:T(512)S(6)} %and.5), kind=kLoop, calls=%fused_computation | loop fusion | flops 248832 | bytes 500261 | tf_op jit(solution)/shard_map/sub | solution.py:37
  60.8 0.7 %slice_reduce_fusion = f32[576]{0:T(1024)S(1)} fusion(f32[8,576]{1,0:T(8,128)} %get-tuple-element.5), kind=kLoop, calls=%fused_computation.3 | loop fusion | bytes 4608 | tf_op jit(solution)/shard_map/slice | solution.py:445
  61.5 0.0 copy-done
  61.5 0.6 sub.11
  (1 shorter events, 0.0 us)
Async XLA Ops:
  1.3 60.2 %copy-start = (f32[576]{0:T(1024)S(1)}, f32[576]{0:T(1024)}, u32[]{:S(2)}) copy-start(f32[576]{0:T(1024)} %param.12) | copy-start | bytes 6916
